TPU v7x, 128 devices: a whole 4x4x4 slice. The times are simulated.
128 devices in a mesh: grp: 2 (over core), tx: 8 (over x_lo, z), ty: 8 (over x_hi, y).
Axes of the slice: x: 4 (x_hi: 2, x_lo: 2; x = x_hi * 2 + x_lo), y: 4, z: 4, core: 2. Of those that a mesh axis runs over, the one named last changes fastest.
Arguments:
- expert_hidden: bfloat16 [2, 64, 8192], P(None, None, 'ty'), may hold values from -400 to 400
- expert_gain: bfloat16 [8192], P('ty'), may hold values from 0.5 to 1.5
- expert_query: bfloat16 [8192, 8192], P('ty', 'tx'), may hold values from -0.0625 to 0.0625
- expert_keys: bfloat16 [8192, 1024], P('ty', 'tx'), may hold values from -0.25 to 0.25
- expert_values: bfloat16 [8192, 1024], P('ty', 'tx'), may hold values from -0.0625 to 0.0625
- expert_output: bfloat16 [8192, 8192], P('tx', 'ty'), may hold values from -0.25 to 0.25
- expert_final: bfloat16 [8192], P('ty'), may hold values from 0.5 to 1.5
- expert_head: bfloat16 [32000, 8192], P(('grp', 'tx'), 'ty'), may hold values from -400 to 400
- expert_keycache: bfloat16 [64, 1024, 1024], P(('grp', 'ty'), None, 'tx'), may hold values from -400 to 400
- expert_valcache: bfloat16 [64, 1024, 1024], P(('grp', 'ty'), None, 'tx'), may hold values from -6 to 6
- amateur_hidden: bfloat16 [2, 64, 4096], P(None, None, 'ty'), may hold values from -400 to 400
- amateur_gain: bfloat16 [4096], P('ty'), may hold values from 0.5 to 1.5
- amateur_query: bfloat16 [4096, 4096], P('ty', 'tx'), may hold values from -0.09375 to 0.09375
- amateur_keys: bfloat16 [4096, 4096], P('ty', 'tx'), may hold values from -0.375 to 0.375
- amateur_values: bfloat16 [4096, 4096], P('ty', 'tx'), may hold values from -0.09375 to 0.09375
- amateur_output: bfloat16 [4096, 4096], P('tx', 'ty'), may hold values from -0.375 to 0.375
- amateur_final: bfloat16 [4096], P('ty'), may hold values from 0.5 to 1.5
- amateur_head: bfloat16 [32000, 4096], P(('grp', 'tx'), 'ty'), may hold values from -400 to 400
- amateur_keycache: bfloat16 [64, 1024, 4096], P(('grp', 'ty'), None, 'tx'), may hold values from -400 to 400
- amateur_valcache: bfloat16 [64, 1024, 4096], P(('grp', 'ty'), None, 'tx'), may hold values from -6 to 6
- lengths: int32 [64], P(('grp', 'ty')), may hold values from 1 to 1022, as said below
- tokens: int32 [2, 64], P(None, 'ty'), may hold values from 0 to 31999
Outputs:
- contrast: float32 [2, 64, 32000], P(None, 'ty', ('grp', 'tx'))
- token_score: float32 [2, 64], P(None, 'ty')
Inputs may be any that keep to these rules, and one draw needn't show every extreme that they name: Row r's prompt fills cache positions 0 to lengths[r] - 1; the later cache positions hold no data.
All inputs are finite; a program needn't handle non-finite values.
Results may differ from a plain program's by a relative error of at most 0.012.
The roundings to bfloat16 on the way count: a program that leaves them out, or rounds other values in their place, can miss the bound.
Values may be sent and summed in bfloat16 or wider, within the bound.
A program may use at most 128 MiB of HBM per device.

v0:
```python
import functools
import math

import jax
import jax.numpy as jnp
from jax import lax
from jax.experimental import pallas as pl
from jax.experimental.pallas import tpu as pltpu
from jax.sharding import PartitionSpec as P

HEAD = 128
EPS = 1e-05
BASE = 10000.0
AMATEUR = 0.5
SCALE = HEAD**-0.5
CHUNK = 512
F32 = jnp.float32
BF16 = jnp.bfloat16
MESH = pl.DeviceIdType.MESH


def iota(shape, axis):
    return lax.broadcasted_iota(jnp.int32, shape, axis)


def mm(a, b):
    return lax.dot_general(a, b, (((1,), (0,)), ((), ())), preferred_element_type=F32)


def mm_t(a, b):
    return lax.dot_general(a, b, (((1,), (1,)), ((), ())), preferred_element_type=F32)


def one_hot(size, source):
    out = iota((size, size), 0)
    return jnp.where(iota((size, size), 1) == source(out), 1.0, 0.0).astype(BF16)


def folded(values):
    half = values.shape[-1] // 2
    return jnp.concatenate([values[..., :half], values[..., half:]], axis=-2)


def unfolded(values):
    return jnp.concatenate([values[..., :8, :], values[..., 8:, :]], axis=-1)


def lane_fold(values):
    total = values[:, :HEAD]
    for start in range(HEAD, values.shape[1], HEAD):
        total = total + values[:, start : start + HEAD]
    return total


def widen(column, width):
    return jnp.concatenate([column] * (width // HEAD), axis=1)


def kernel(axes, dims, *refs):
    n_grp, n_tx, n_ty = axes
    (
        hid_e, gain_e, wq_e, wk_e, wv_e, wo_e, fin_e, head_e, kc_e, vc_e,
        hid_a, gain_a, wq_a, wk_a, wv_a, wo_a, fin_a, head_a, kc_a, vc_a,
        h_lengths, h_tokens,
        out_ref, score_ref,
        lengths, tokens, v_gain_e, v_fin_e, v_gain_a, v_fin_a,
        v_hid_e, v_wq_e, v_wk_e, v_wv_e, v_wo_e, v_head_e, v_kc_e, v_vc_e,
        v_hid_a, v_wq_a, v_wk_a, v_wv_a, v_wo_a, v_head_a, v_kc_a, v_vc_a,
        x_e, x_a, sq_send, sq_recv,
        p_send_e, p_recv_e, p_send_a, p_recv_a,
        g_e, g_a,
        o_send_e, o_recv_e, o_send_a, o_recv_a,
        s_send_e, s_recv_e, s_send_a, s_recv_a,
        f_e, f_a, rows_e, rows_a,
        l_send, l_recv, t_send, t_recv,
        local_sem, ty_send, ty_recv, tx_send, tx_recv, fw_send, fw_recv, l_ssem, l_rsem, t_ssem, t_rsem,
    ) = refs
    grp, tx, ty = lax.axis_index("grp"), lax.axis_index("tx"), lax.axis_index("ty")
    half_rows = v_hid_e.shape[1]
    width_e, width_a = v_hid_e.shape[2], v_hid_a.shape[2]
    heads_e, heads_a = v_wq_e.shape[1] // HEAD, v_wq_a.shape[1] // HEAD
    vocab = head_e.shape[0]

    first = pl.multiple_of(grp * half_rows, half_rows)
    pairs = [
        (hid_e.at[:, pl.ds(first, half_rows)], v_hid_e),
        (hid_a.at[:, pl.ds(first, half_rows)], v_hid_a),
        (h_lengths, lengths), (gain_e, v_gain_e), (gain_a, v_gain_a),
        (fin_e, v_fin_e), (fin_a, v_fin_a), (h_tokens, tokens),
        (wq_e, v_wq_e), (wk_e, v_wk_e), (wv_e, v_wv_e),
        (wq_a, v_wq_a), (wk_a, v_wk_a), (wv_a, v_wv_a),
        (kc_e, v_kc_e), (vc_e, v_vc_e), (kc_a, v_kc_a), (vc_a, v_vc_a),
        (wo_e, v_wo_e), (wo_a, v_wo_a),
        (head_e, v_head_e.at[pl.ds(0, vocab)]), (head_a, v_head_a.at[pl.ds(0, vocab)]),
    ]
    loads = [
        pltpu.make_async_copy(source, target, local_sem.at[number])
        for number, (source, target) in enumerate(pairs)
    ]
    for load in loads[:8]:
        load.start()
    (l_hid_e, l_hid_a, l_lengths, l_gain_e, l_gain_a, l_fin_e, l_fin_a, l_tokens, l_wq_e, l_wk_e, l_wv_e, l_wq_a, l_wk_a, l_wv_a,
     l_kc_e, l_vc_e, l_kc_a, l_vc_a, l_wo_e, l_wo_a, l_head_e, l_head_a) = loads

    def ty_peer(step):
        return lax.rem(ty + step, n_ty)

    def tx_peer(step):
        return lax.rem(tx + step, n_tx)

    flat = grp * n_tx + tx
    n_flat = n_grp * n_tx

    def flat_peer(step):
        peer = lax.rem(flat + step, n_flat)
        return {"grp": peer // n_tx, "tx": lax.rem(peer, n_tx)}

    barrier = pltpu.get_barrier_semaphore()
    for step in range(1, n_ty):
        pl.semaphore_signal(barrier, inc=1, device_id={"ty": ty_peer(step)}, device_id_type=MESH)
    for step in range(1, n_flat):
        pl.semaphore_signal(barrier, inc=1, device_id=flat_peer(step), device_id_type=MESH)

    for load in loads[8:14]:
        load.start()

    sent = []

    def push(source, target, send_sem, recv_sem, device):
        copy = pltpu.make_async_remote_copy(
            src_ref=source, dst_ref=target, send_sem=send_sem, recv_sem=recv_sem,
            device_id=device, device_id_type=MESH,
        )
        copy.start()
        sent.append(copy)
        return copy

    n_rows = 2 * half_rows
    block = half_rows // n_ty
    order = one_hot(
        n_rows, lambda o: (o // block) % 2 * half_rows + o // (2 * block) * block + o % block
    )
    l_hid_e.wait()
    wide_e = mm(order, v_hid_e[...].reshape(n_rows, width_e))
    x_e[...] = wide_e.reshape(n_ty, 8, width_e)
    l_hid_a.wait()
    wide_a = mm(order, v_hid_a[...].reshape(n_rows, width_a))
    x_a[...] = wide_a.reshape(n_ty, 8, width_a)
    partial = jnp.concatenate([lane_fold(wide_e * wide_e), lane_fold(wide_a * wide_a)], axis=0)
    own = jnp.broadcast_to(jnp.sum(partial.T, axis=0, keepdims=True), (8, HEAD))
    sq_send[...] = own

    pl.semaphore_wait(barrier, n_ty - 1 + n_flat - 1)

    copies = [
        push(sq_send, sq_recv.at[step], ty_send.at[0, step], ty_recv.at[0, step], {"ty": ty_peer(step)})
        for step in range(1, n_ty)
    ]

    for load in loads[14:18]:
        load.start()

    row8, lane8 = iota((8, HEAD), 0), iota((8, HEAD), 1)
    position = jnp.zeros((8, HEAD), jnp.int32)
    l_lengths.wait()
    for i in range(block):
        position = jnp.where(row8 % block == i, lengths[i], position)
    position = (position + row8 // block).astype(F32)
    exponent = (lane8 % (HEAD // 2)).astype(F32) * (2.0 / HEAD)
    angle = position * jnp.exp(exponent * (-math.log(BASE)))
    cosine = jnp.cos(angle)
    sine = jnp.where(lane8 < HEAD // 2, -1.0, 1.0) * jnp.sin(angle)

    def rotated(values):
        turned = jnp.concatenate([values[:, HEAD // 2 :], values[:, : HEAD // 2]], axis=1)
        return values * cosine + turned * sine

    total = own
    for copy, step in zip(copies, range(1, n_ty)):
        copy.wait_recv()
        total = total + sq_recv[step]
    square = jnp.broadcast_to(total[0:1], (HEAD, HEAD)).T
    root_e = lax.rsqrt(square[:n_rows] / (width_e * n_ty) + EPS)
    root_a = lax.rsqrt(square[n_rows:] / (width_a * n_ty) + EPS)

    def project(x, root, g_load, gain, weights, send, recv, kind):
        width = x.shape[2]
        g_load.wait()
        values = x[...].reshape(n_rows, width)
        normed = (values * widen(root, width) * gain[...].astype(F32).reshape(1, width)).astype(BF16)
        parts = []
        for load, weight in weights:
            load.wait()
            columns = weight.shape[1]
            for at in range(0, columns, CHUNK):
                parts.append(mm(normed, weight[:, at : at + min(CHUNK, columns - at)]))
        send[...] = folded(jnp.concatenate(parts, axis=1).reshape(n_ty, 8, 2 * send.shape[2])).astype(BF16)
        return [
            push(send.at[ty_peer(step)], recv.at[step], ty_send.at[kind, step], ty_recv.at[kind, step],
                 {"ty": ty_peer(step)})
            for step in range(1, n_ty)
        ]

    sent_pe = project(x_e, root_e, l_gain_e, v_gain_e, ((l_wq_e, v_wq_e), (l_wk_e, v_wk_e), (l_wv_e, v_wv_e)), p_send_e, p_recv_e, 1)
    sent_pa = project(x_a, root_a, l_gain_a, v_gain_a, ((l_wq_a, v_wq_a), (l_wk_a, v_wk_a), (l_wv_a, v_wv_a)), p_send_a, p_recv_a, 2)

    for load in loads[18:]:
        load.start()

    def summed(copies, send, recv, me):
        total = send[me].astype(F32)
        for copy, step in zip(copies, range(1, n_ty)):
            copy.wait_recv()
            total = total + recv[step].astype(F32)
        return unfolded(total)

    def padded(rows, size):
        if rows.shape[0] == size:
            return rows
        return jnp.concatenate([rows, jnp.zeros((size - rows.shape[0], rows.shape[1]), F32)], axis=0)

    def attend(acc, heads, key_heads, k_load, keys, v_load, values):
        group = heads // key_heads
        n_query = heads * 8
        per_row = 2 * heads
        cache = keys.shape[1]
        wide = key_heads * HEAD
        query = jnp.concatenate([rotated(acc[:, h * HEAD : (h + 1) * HEAD]) for h in range(heads)], axis=0)
        at = heads * HEAD
        fresh_k = jnp.concatenate(
            [rotated(acc[:, at + h * HEAD : at + (h + 1) * HEAD]) for h in range(key_heads)], axis=0
        )
        at += wide
        fresh_v = jnp.concatenate(
            [acc[:, at + h * HEAD : at + (h + 1) * HEAD] for h in range(key_heads)], axis=0
        )
        fresh_k = padded(fresh_k, HEAD).astype(BF16)
        fresh_v = padded(fresh_v, HEAD).astype(BF16)
        forth = one_hot(n_query, lambda o: o % heads * 8 + o // heads % 2 * block + o // per_row)
        back = one_hot(n_query, lambda o: o % block * per_row + o // block % 2 * heads + o // 8)
        query = mm(forth, query.astype(BF16))
        owner = iota((n_query, HEAD), 0)
        lane = iota((n_query, HEAD), 1)
        fresh = mm_t(query.astype(BF16), fresh_k) * SCALE
        seen = (
            (lane < key_heads * 8)
            & (lane // 8 == owner % heads // group)
            & (lane % block == owner // per_row)
            & (lane // block % 2 <= owner // heads % 2)
        )
        fresh = jnp.where(seen, fresh, -jnp.inf)
        if key_heads > 1:
            spread = widen(query, wide)
            keep = iota((n_query, wide), 1) // HEAD == iota((n_query, wide), 0) % heads // group
            query = jnp.where(keep, spread, 0.0)
        k_load.wait()
        cached = []
        for i in range(block):
            part = query[i * per_row : (i + 1) * per_row].astype(BF16)
            score = mm_t(part, keys[i]) * SCALE
            cached.append(jnp.where(iota((per_row, cache), 1) < lengths[i], score, -jnp.inf))
        cached = jnp.concatenate(cached, axis=0)
        peak = jnp.maximum(jnp.max(cached, axis=1, keepdims=True), jnp.max(fresh, axis=1, keepdims=True))
        cached = jnp.exp(cached - peak)
        fresh = jnp.exp(fresh - peak)
        total = jnp.sum(cached, axis=1, keepdims=True) + jnp.sum(fresh, axis=1, keepdims=True)
        v_load.wait()
        mixture = jnp.concatenate(
            [mm(cached[i * per_row : (i + 1) * per_row].astype(BF16), values[i]) for i in range(block)], axis=0
        )
        if key_heads > 1:
            picked = jnp.zeros((n_query, HEAD), F32)
            for h in range(key_heads):
                picked = picked + jnp.where(owner % heads // group == h, mixture[:, h * HEAD : (h + 1) * HEAD], 0.0)
            mixture = picked
        mixture = mixture + mm(fresh.astype(BF16), fresh_v)
        ready = mm(back, (mixture / total).astype(BF16))
        return jnp.concatenate([ready[h * 8 : (h + 1) * 8] for h in range(heads)], axis=1)

    def gather(rows, buffer, kind):
        buffer[ty] = folded(rows).astype(BF16)
        return [
            push(buffer.at[ty], buffer.at[ty], ty_send.at[kind, step], ty_recv.at[kind, step], {"ty": ty_peer(step)})
            for step in range(1, n_ty)
        ]

    acc = summed(sent_pe, p_send_e, p_recv_e, ty)
    sent_ge = gather(attend(acc, heads_e, v_wk_e.shape[1] // HEAD, l_kc_e, v_kc_e, l_vc_e, v_vc_e), g_e, 3)
    acc = summed(sent_pa, p_send_a, p_recv_a, ty)
    sent_ga = gather(attend(acc, heads_a, v_wk_a.shape[1] // HEAD, l_kc_a, v_kc_a, l_vc_a, v_vc_a), g_a, 4)

    def output(copies, buffer, load, weight, send, recv, kind):
        for copy in copies:
            copy.wait_recv()
        rows = unfolded(buffer[...].astype(F32)).reshape(n_rows, weight.shape[0]).astype(BF16)
        load.wait()
        columns = weight.shape[1]
        parts = [mm(rows, weight[:, at : at + CHUNK]) for at in range(0, columns, CHUNK)]
        send[...] = folded(jnp.concatenate(parts, axis=1).reshape(n_tx, 8, columns)).astype(BF16)
        return [
            push(send.at[tx_peer(step)], recv.at[step], tx_send.at[kind, step], tx_recv.at[kind, step],
                 {"tx": tx_peer(step)})
            for step in range(1, n_tx)
        ]

    sent_oe = output(sent_ge, g_e, l_wo_e, v_wo_e, o_send_e, o_recv_e, 0)
    sent_oa = output(sent_ga, g_a, l_wo_a, v_wo_a, o_send_a, o_recv_a, 1)

    def residual(copies, x, send, recv, s_send, s_recv, kind):
        values = x[tx] + summed(copies, send, recv, tx)
        part = lane_fold(values * values)
        s_send[...] = part
        return values, part, [
            push(s_send, s_recv.at[step], ty_send.at[kind, step], ty_recv.at[kind, step], {"ty": ty_peer(step)})
            for step in range(1, n_ty)
        ]

    res_e, part_e, sent_se = residual(sent_oe, x_e, o_send_e, o_recv_e, s_send_e, s_recv_e, 5)
    res_a, part_a, sent_sa = residual(sent_oa, x_a, o_send_a, o_recv_a, s_send_a, s_recv_a, 6)

    partner = {"grp": 1 - grp}

    def final(values, part, copies, s_recv, g_load, gain, buffer, kind):
        width = values.shape[1]
        g_load.wait()
        for copy, step in zip(copies, range(1, n_ty)):
            copy.wait_recv()
            part = part + s_recv[step]
        mean = jnp.sum(part, axis=1, keepdims=True) / (width * n_ty)
        rows = values * lax.rsqrt(mean + EPS) * gain[...].astype(F32).reshape(1, width)
        buffer[flat] = folded(rows).astype(BF16)
        across = [
            push(buffer.at[flat], buffer.at[flat], tx_send.at[kind, step], tx_recv.at[kind, step], {"tx": tx_peer(step)})
            for step in range(1, n_tx)
        ]
        forward = [
            push(buffer.at[flat], buffer.at[flat], fw_send.at[kind - 2, 0], fw_recv.at[kind - 2, 0], partner)
        ]
        return across, forward

    def pass_on(across, forward, buffer, kind):
        for copy, step in zip(across, range(1, n_tx)):
            copy.wait_recv()
            source = grp * n_tx + lax.rem(tx + n_tx - step, n_tx)
            forward.append(
                push(buffer.at[source], buffer.at[source], fw_send.at[kind - 2, step], fw_recv.at[kind - 2, step], partner)
            )

    def collect(forward, buffer, rows):
        for copy in forward:
            copy.wait_recv()
        rows[...] = unfolded(buffer[...].astype(F32)).reshape(rows.shape).astype(BF16)

    across_e, forward_e = final(res_e, part_e, sent_se, s_recv_e, l_fin_e, v_fin_e, f_e, 2)
    across_a, forward_a = final(res_a, part_a, sent_sa, s_recv_a, l_fin_a, v_fin_a, f_a, 3)

    padding = v_head_e.shape[0] - vocab
    l_head_e.wait()
    v_head_e[pl.ds(vocab, padding), :] = jnp.zeros((padding, width_e), BF16)
    l_head_a.wait()
    v_head_a[pl.ds(vocab, padding), :] = jnp.zeros((padding, width_a), BF16)

    n_chunk = v_head_e.shape[0] // CHUNK
    logit_copies = []

    def logits(rows, head, base):
        for c in range(n_chunk):
            part = mm_t(rows[...], head[pl.ds(c * CHUNK, CHUNK), :])
            l_send[base + c] = part.reshape(n_ty, 16, CHUNK).astype(BF16)
            for step in range(1, n_ty):
                logit_copies.append(
                    push(l_send.at[base + c, ty_peer(step)], l_recv.at[base + c, step],
                         l_ssem.at[base + c, step], l_rsem.at[base + c, step], {"ty": ty_peer(step)})
                )

    pass_on(across_e, forward_e, f_e, 2)
    collect(forward_e, f_e, rows_e)
    logits(rows_e, v_head_e, 0)
    pass_on(across_a, forward_a, f_a, 3)
    collect(forward_a, f_a, rows_a)
    logits(rows_a, v_head_a, n_chunk)

    def chunk_sum(c):
        total = l_send[c, ty].astype(F32)
        for step in range(1, n_ty):
            logit_copies[c * (n_ty - 1) + step - 1].wait_recv()
            total = total + l_recv[c, step].astype(F32)
        return total

    lane_c = iota((16, CHUNK), 1)

    def peak_and_total(parts):
        masked = [jnp.where(lane_c + c * CHUNK < vocab, part, -jnp.inf) for c, part in enumerate(parts)]
        peak = masked[0]
        for part in masked[1:]:
            peak = jnp.maximum(peak, part)
        peak = jnp.max(peak, axis=1, keepdims=True)
        total = jnp.exp(masked[0] - peak)
        for part in masked[1:]:
            total = total + jnp.exp(part - peak)
        return peak, jnp.sum(total, axis=1, keepdims=True)

    l_tokens.wait()
    row16 = iota((16, HEAD), 0)
    token = jnp.zeros((16, HEAD), jnp.int32)
    for s in range(2):
        for r in range(8):
            token = jnp.where(row16 == r // block * 8 + s * block + r % block, tokens[s, r], token)
    token = widen(token - flat * vocab, CHUNK)

    expert = [chunk_sum(c) for c in range(n_chunk)]
    peak_e, total_e = peak_and_total(expert)
    amateur = [chunk_sum(n_chunk + c) for c in range(n_chunk)]
    peak_a, total_a = peak_and_total(amateur)
    chosen = jnp.zeros((16, CHUNK), F32)
    mixed = []
    for c in range(n_chunk):
        mixed.append(expert[c] - AMATEUR * amateur[c])
        column = lane_c + c * CHUNK
        chosen = chosen + jnp.where((column == token) & (column < vocab), mixed[c], 0.0)
    chosen = jnp.sum(chosen, axis=1, keepdims=True)

    lane16 = iota((16, HEAD), 1) % 64
    tile = jnp.where(lane16 == 0, peak_e, jnp.where(lane16 == 1, total_e, 0.0))
    tile = jnp.where(lane16 == 2, peak_a, jnp.where(lane16 == 3, total_a, tile))
    tile = jnp.where(lane16 == 4, chosen, tile)
    tile = jnp.where(lane8 < 64, tile[:8], tile[8:])
    t_send[...] = tile
    copies = [
        push(t_send, t_recv.at[step], t_ssem.at[step], t_rsem.at[step], flat_peer(step)) for step in range(1, n_flat)
    ]
    for copy in copies:
        copy.wait_recv()
    tiles = [tile] + [t_recv[step] for step in range(1, n_flat)]
    highest = functools.reduce(jnp.maximum, tiles)
    picked = functools.reduce(jnp.add, tiles)

    def shifted(values):
        return jnp.concatenate([values[:, 1:], values[:, :1]], axis=1)

    summed_up = functools.reduce(jnp.add, [jnp.exp(t - highest) * shifted(t) for t in tiles])
    log_total = highest + jnp.log(summed_up)

    def column(values, lane):
        return jnp.concatenate([values[:, lane : lane + 1], values[:, lane + 64 : lane + 65]], axis=0)

    offset = column(log_total, 0) - AMATEUR * column(log_total, 2)
    for c in range(n_chunk):
        size = min(CHUNK, vocab - c * CHUNK)
        contrast = mixed[c] - offset
        for s in range(2):
            low = s * block
            out_ref[s, :, c * CHUNK : c * CHUNK + size] = jnp.concatenate(
                [contrast[low : low + block], contrast[8 + low : 8 + low + block]], axis=0
            )[:, :size]
    value = jnp.broadcast_to(column(picked, 4) - offset, (16, HEAD))
    lane_r = iota((16, HEAD), 1)
    for s in range(2):
        mine = row16 == lane_r // block * 8 + s * block + lane_r % block
        line = jnp.sum(jnp.where(mine & (lane_r < 8), value, 0.0), axis=0, keepdims=True)
        score_ref[s : s + 1, :] = line[:, :8]

    for copy in sent:
        copy.wait_send()


def on_device(axes, *args):
    (
        hid_e, gain_e, wq_e, wk_e, wv_e, wo_e, fin_e, head_e, kc_e, vc_e,
        hid_a, gain_a, wq_a, wk_a, wv_a, wo_a, fin_a, head_a, kc_a, vc_a,
        lengths, tokens,
    ) = args
    n_grp, n_tx, n_ty = axes
    n_flat = n_grp * n_tx
    half = hid_e.shape[1] // n_grp
    vocab = head_e.shape[0]
    padded = -(-vocab // CHUNK) * CHUNK
    n_chunk = padded // CHUNK
    n_rows = 2 * half
    width_e, width_a = hid_e.shape[2], hid_a.shape[2]
    cols_e = wq_e.shape[1] + wk_e.shape[1] + wv_e.shape[1]
    cols_a = wq_a.shape[1] + wk_a.shape[1] + wv_a.shape[1]
    inner_e, inner_a = wo_e.shape[0], wo_a.shape[0]

    def like(array):
        return pltpu.VMEM(array.shape, array.dtype)

    scratch = [
        pltpu.SMEM(lengths.shape, jnp.int32), pltpu.SMEM(tokens.shape, jnp.int32),
        like(gain_e), like(fin_e), like(gain_a), like(fin_a),
    ]
    for hid, wq, wk, wv, wo, head, kc, vc in (
        (hid_e, wq_e, wk_e, wv_e, wo_e, head_e, kc_e, vc_e),
        (hid_a, wq_a, wk_a, wv_a, wo_a, head_a, kc_a, vc_a),
    ):
        scratch += [
            pltpu.VMEM((2, half, hid.shape[2]), BF16), like(wq), like(wk), like(wv), like(wo),
            pltpu.VMEM((padded, head.shape[1]), BF16), like(kc), like(vc),
        ]
    scratch += [
        pltpu.VMEM((n_ty, 8, width_e), F32), pltpu.VMEM((n_ty, 8, width_a), F32),
        pltpu.VMEM((8, HEAD), F32), pltpu.VMEM((n_ty, 8, HEAD), F32),
        pltpu.VMEM((n_ty, 16, cols_e // 2), BF16), pltpu.VMEM((n_ty, 16, cols_e // 2), BF16),
        pltpu.VMEM((n_ty, 16, cols_a // 2), BF16), pltpu.VMEM((n_ty, 16, cols_a // 2), BF16),
        pltpu.VMEM((n_ty, 16, inner_e // 2), BF16), pltpu.VMEM((n_ty, 16, inner_a // 2), BF16),
        pltpu.VMEM((n_tx, 16, width_e // 2), BF16), pltpu.VMEM((n_tx, 16, width_e // 2), BF16),
        pltpu.VMEM((n_tx, 16, width_a // 2), BF16), pltpu.VMEM((n_tx, 16, width_a // 2), BF16),
        pltpu.VMEM((8, HEAD), F32), pltpu.VMEM((n_ty, 8, HEAD), F32),
        pltpu.VMEM((8, HEAD), F32), pltpu.VMEM((n_ty, 8, HEAD), F32),
        pltpu.VMEM((n_flat, 16, width_e // 2), BF16), pltpu.VMEM((n_flat, 16, width_a // 2), BF16),
        pltpu.VMEM((n_flat * 8, width_e), BF16), pltpu.VMEM((n_flat * 8, width_a), BF16),
        pltpu.VMEM((2 * n_chunk, n_ty, 16, CHUNK), BF16), pltpu.VMEM((2 * n_chunk, n_ty, 16, CHUNK), BF16),
        pltpu.VMEM((8, HEAD), F32), pltpu.VMEM((n_flat, 8, HEAD), F32),
        pltpu.SemaphoreType.DMA((22,)),
        pltpu.SemaphoreType.DMA((7, n_ty)), pltpu.SemaphoreType.DMA((7, n_ty)),
        pltpu.SemaphoreType.DMA((4, n_tx)), pltpu.SemaphoreType.DMA((4, n_tx)),
        pltpu.SemaphoreType.DMA((2, n_tx)), pltpu.SemaphoreType.DMA((2, n_tx)),
        pltpu.SemaphoreType.DMA((2 * n_chunk, n_ty)), pltpu.SemaphoreType.DMA((2 * n_chunk, n_ty)),
        pltpu.SemaphoreType.DMA((n_flat,)), pltpu.SemaphoreType.DMA((n_flat,)),
    ]
    hbm = pl.BlockSpec(memory_space=pl.ANY)
    vmem = pl.BlockSpec(memory_space=pltpu.VMEM)
    macs = n_rows * (width_e * (cols_e + inner_e) + width_a * (cols_a + inner_a)) + 2 * n_rows * vocab * (width_e + width_a)
    read = sum(array.size * array.dtype.itemsize for array in args)
    return pl.pallas_call(
        functools.partial(kernel, axes, None),
        out_shape=(
            jax.ShapeDtypeStruct((2, hid_e.shape[1] // n_ty, vocab), F32),
            jax.ShapeDtypeStruct((2, hid_e.shape[1] // n_ty), F32),
        ),
        in_specs=[hbm] * len(args),
        out_specs=(vmem, vmem),
        scratch_shapes=scratch,
        compiler_params=pltpu.CompilerParams(
            collective_id=0, has_side_effects=True, vmem_limit_bytes=56 * 1024 * 1024
        ),
        cost_estimate=pl.CostEstimate(flops=2 * macs, bytes_accessed=read, transcendentals=0),
        name="contrast",
    )(*args)


def solution(mesh):
    model = (
        P(None, None, "ty"), P("ty"), P("ty", "tx"), P("ty", "tx"), P("ty", "tx"), P("tx", "ty"), P("ty"),
        P(("grp", "tx"), "ty"), P(("grp", "ty"), None, "tx"), P(("grp", "ty"), None, "tx"),
    )
    axes = tuple(mesh.shape[name] for name in ("grp", "tx", "ty"))
    return jax.shard_map(
        functools.partial(on_device, axes),
        mesh=mesh,
        in_specs=model + model + (P(("grp", "ty")), P(None, "ty")),
        out_specs=(P(None, "ty", ("grp", "tx")), P(None, "ty")),
        check_vma=False,
    )
```

profile of v0, /device:TPU:1, one launch (start us, length us, event | category | flops | bytes accessed | tf_op | source)
XLA Modules:
  0.0 67.4 jit_solution(17591127543382744711)
XLA Ops:
  0.6 64.0 %contrast.1 = (f32[2,8,2000]{2,1,0:T(8,128)}, f32[2,8]{1,0:T(2,128)}) custom-call(bf16[2,64,1024]{2,1,0:T(8,128)(2,1)} %refs_0_.1, bf16[1024]{0:T(1024)(128)(2,1)} %refs_1_.1, bf16[1024,1024]{1,0:T(8,128)(2,1)} %refs_2_.1, bf16[1024,128]{1,0:T(8,128)(2,1)} %refs_3_.1, bf16[1024,128]{1,0:T(8,128)(2,1)} %refs_4_.1, bf16[1024,1024]{1,0:T(8,128)(2,1)} %refs_5_.1, ...), custom_call_target="tpu_custom_call" | custom-call | flops 1222639616 | bytes 23844944 | tf_op jit(solution)/shard_map/contrast/pallas_call | solution.py:525
  64.6 1.6 %copy.26 = f32[2,8,2000]{2,1,0:T(8,128)} copy(f32[2,8,2000]{2,1,0:T(8,128)} %get-tuple-element.4) | data formatting | bytes 256000
  66.2 1.2 %copy.27 = f32[2,8]{1,0:T(2,128)} copy(f32[2,8]{1,0:T(2,128)} %get-tuple-element.5) | data formatting | bytes 128
where the time goes:
time: 67.6 us; the launch traced here: 67.4 us
  Pallas kernels  64 us (95%)
  local copies, waits for them, and re-layouts  2.8 us (4%)
    pallas_call x1, Pallas kernels, on_device(): pl.pallas_call(functools.partial(kernel, axes, None), out_shape=(jax.Shap...  64 us
    unnamed x2, local copies, waits for them, and re-layouts  2.8 us

commit v1 on v0

--- a/solution.py
+++ b/solution.py
@@ -14,6 +14,7 @@
 AMATEUR = 0.5
 SCALE = HEAD**-0.5
 CHUNK = 512
+SLAB = 1024
 F32 = jnp.float32
 BF16 = jnp.bfloat16
 MESH = pl.DeviceIdType.MESH
@@ -43,6 +44,10 @@
 
 def unfolded(values):
     return jnp.concatenate([values[..., :8, :], values[..., 8:, :]], axis=-1)
+
+
+def packed(values, ref):
+    return values if ref.dtype == F32 else folded(values).astype(ref.dtype)
 
 
 def lane_fold(values):
@@ -103,37 +108,73 @@
      l_kc_e, l_vc_e, l_kc_a, l_vc_a, l_wo_e, l_wo_a, l_head_e, l_head_a) = loads
 
     def ty_peer(step):
-        return lax.rem(ty + step, n_ty)
+        return lax.rem(ty // 4 + step // 4, n_ty // 4) * 4 + lax.rem(ty + step, 4)
 
     def tx_peer(step):
-        return lax.rem(tx + step, n_tx)
+        return lax.rem(tx // 4 + step // 4, n_tx // 4) * 4 + lax.rem(tx + step, 4)
 
     flat = grp * n_tx + tx
     n_flat = n_grp * n_tx
 
     def flat_peer(step):
-        peer = lax.rem(flat + step, n_flat)
-        return {"grp": peer // n_tx, "tx": lax.rem(peer, n_tx)}
+        return {"grp": lax.rem(grp + step // n_tx, n_grp), "tx": tx_peer(lax.rem(step, n_tx))}
+
+    def to_ty(step):
+        return {"ty": ty_peer(step)}
+
+    def to_tx(step):
+        return {"tx": tx_peer(step)}
 
     barrier = pltpu.get_barrier_semaphore()
-    for step in range(1, n_ty):
-        pl.semaphore_signal(barrier, inc=1, device_id={"ty": ty_peer(step)}, device_id_type=MESH)
-    for step in range(1, n_flat):
-        pl.semaphore_signal(barrier, inc=1, device_id=flat_peer(step), device_id_type=MESH)
+
+    def greet(device):
+        pl.semaphore_signal(barrier, inc=1, device_id=device, device_id_type=MESH)
+
+    @pl.loop(1, n_ty)
+    def _(step):
+        greet(to_ty(n_ty - step))
+
+    @pl.loop(1, n_flat)
+    def _(step):
+        greet(flat_peer(n_flat - step))
 
     for load in loads[8:14]:
         load.start()
 
-    sent = []
-
-    def push(source, target, send_sem, recv_sem, device):
-        copy = pltpu.make_async_remote_copy(
-            src_ref=source, dst_ref=target, send_sem=send_sem, recv_sem=recv_sem,
-            device_id=device, device_id_type=MESH,
-        )
-        copy.start()
-        sent.append(copy)
-        return copy
+    started = []
+
+    class Exchange:
+        def __init__(self, n, source, target, send_sems, recv_sems, device, begin=True):
+            self.n = n
+            self.make = lambda step: pltpu.make_async_remote_copy(
+                src_ref=source(step), dst_ref=target(step), send_sem=send_sems.at[step], recv_sem=recv_sems.at[step],
+                device_id=device(step), device_id_type=MESH,
+            )
+            started.append(self)
+            if begin:
+                self.begin()
+
+        def begin(self):
+            @pl.loop(1, self.n)
+            def _(step):
+                self.make(self.n - step).start()
+
+        def arrive(self):
+            @pl.loop(1, self.n)
+            def _(step):
+                self.make(step).wait_recv()
+
+        def finish(self):
+            @pl.loop(1, self.n)
+            def _(step):
+                self.make(step).wait_send()
+
+    def add_up(exchange, first, recv):
+        def body(step, total):
+            exchange.make(step).wait_recv()
+            return total + recv[step].astype(F32)
+
+        return lax.fori_loop(1, exchange.n, body, first)
 
     n_rows = 2 * half_rows
     block = half_rows // n_ty
@@ -152,11 +193,7 @@
 
     pl.semaphore_wait(barrier, n_ty - 1 + n_flat - 1)
 
-    copies = [
-        push(sq_send, sq_recv.at[step], ty_send.at[0, step], ty_recv.at[0, step], {"ty": ty_peer(step)})
-        for step in range(1, n_ty)
-    ]
-
+    squares = Exchange(n_ty, lambda d: sq_send, lambda d: sq_recv.at[d], ty_send.at[0], ty_recv.at[0], to_ty)
     for load in loads[14:18]:
         load.start()
 
@@ -175,10 +212,7 @@
         turned = jnp.concatenate([values[:, HEAD // 2 :], values[:, : HEAD // 2]], axis=1)
         return values * cosine + turned * sine
 
-    total = own
-    for copy, step in zip(copies, range(1, n_ty)):
-        copy.wait_recv()
-        total = total + sq_recv[step]
+    total = add_up(squares, own, sq_recv)
     square = jnp.broadcast_to(total[0:1], (HEAD, HEAD)).T
     root_e = lax.rsqrt(square[:n_rows] / (width_e * n_ty) + EPS)
     root_a = lax.rsqrt(square[n_rows:] / (width_a * n_ty) + EPS)
@@ -194,12 +228,8 @@
             columns = weight.shape[1]
             for at in range(0, columns, CHUNK):
                 parts.append(mm(normed, weight[:, at : at + min(CHUNK, columns - at)]))
-        send[...] = folded(jnp.concatenate(parts, axis=1).reshape(n_ty, 8, 2 * send.shape[2])).astype(BF16)
-        return [
-            push(send.at[ty_peer(step)], recv.at[step], ty_send.at[kind, step], ty_recv.at[kind, step],
-                 {"ty": ty_peer(step)})
-            for step in range(1, n_ty)
-        ]
+        send[...] = packed(jnp.concatenate(parts, axis=1).reshape(n_ty, 8, -1), send)
+        return Exchange(n_ty, lambda d: send.at[ty_peer(d)], lambda d: recv.at[d], ty_send.at[kind], ty_recv.at[kind], to_ty)
 
     sent_pe = project(x_e, root_e, l_gain_e, v_gain_e, ((l_wq_e, v_wq_e), (l_wk_e, v_wk_e), (l_wv_e, v_wv_e)), p_send_e, p_recv_e, 1)
     sent_pa = project(x_a, root_a, l_gain_a, v_gain_a, ((l_wq_a, v_wq_a), (l_wk_a, v_wk_a), (l_wv_a, v_wv_a)), p_send_a, p_recv_a, 2)
@@ -207,12 +237,9 @@
     for load in loads[18:]:
         load.start()
 
-    def summed(copies, send, recv, me):
-        total = send[me].astype(F32)
-        for copy, step in zip(copies, range(1, n_ty)):
-            copy.wait_recv()
-            total = total + recv[step].astype(F32)
-        return unfolded(total)
+    def summed(exchange, send, recv, me):
+        total = add_up(exchange, send[me].astype(F32), recv)
+        return total if send.dtype == F32 else unfolded(total)
 
     def padded(rows, size):
         if rows.shape[0] == size:
@@ -279,80 +306,71 @@
 
     def gather(rows, buffer, kind):
         buffer[ty] = folded(rows).astype(BF16)
-        return [
-            push(buffer.at[ty], buffer.at[ty], ty_send.at[kind, step], ty_recv.at[kind, step], {"ty": ty_peer(step)})
-            for step in range(1, n_ty)
-        ]
+        return Exchange(n_ty, lambda d: buffer.at[ty], lambda d: buffer.at[ty], ty_send.at[kind], ty_recv.at[kind], to_ty)
 
     acc = summed(sent_pe, p_send_e, p_recv_e, ty)
     sent_ge = gather(attend(acc, heads_e, v_wk_e.shape[1] // HEAD, l_kc_e, v_kc_e, l_vc_e, v_vc_e), g_e, 3)
     acc = summed(sent_pa, p_send_a, p_recv_a, ty)
     sent_ga = gather(attend(acc, heads_a, v_wk_a.shape[1] // HEAD, l_kc_a, v_kc_a, l_vc_a, v_vc_a), g_a, 4)
 
-    def output(copies, buffer, load, weight, send, recv, kind):
-        for copy in copies:
-            copy.wait_recv()
+    def output(exchange, buffer, load, weight, send, recv, kind):
+        exchange.arrive()
         rows = unfolded(buffer[...].astype(F32)).reshape(n_rows, weight.shape[0]).astype(BF16)
         load.wait()
         columns = weight.shape[1]
         parts = [mm(rows, weight[:, at : at + CHUNK]) for at in range(0, columns, CHUNK)]
-        send[...] = folded(jnp.concatenate(parts, axis=1).reshape(n_tx, 8, columns)).astype(BF16)
-        return [
-            push(send.at[tx_peer(step)], recv.at[step], tx_send.at[kind, step], tx_recv.at[kind, step],
-                 {"tx": tx_peer(step)})
-            for step in range(1, n_tx)
-        ]
+        send[...] = packed(jnp.concatenate(parts, axis=1).reshape(n_tx, 8, columns), send)
+        return Exchange(n_tx, lambda d: send.at[tx_peer(d)], lambda d: recv.at[d], tx_send.at[kind], tx_recv.at[kind], to_tx)
 
     sent_oe = output(sent_ge, g_e, l_wo_e, v_wo_e, o_send_e, o_recv_e, 0)
     sent_oa = output(sent_ga, g_a, l_wo_a, v_wo_a, o_send_a, o_recv_a, 1)
 
-    def residual(copies, x, send, recv, s_send, s_recv, kind):
-        values = x[tx] + summed(copies, send, recv, tx)
+    def residual(exchange, x, send, recv, s_send, s_recv, kind):
+        values = x[tx] + summed(exchange, send, recv, tx)
         part = lane_fold(values * values)
         s_send[...] = part
-        return values, part, [
-            push(s_send, s_recv.at[step], ty_send.at[kind, step], ty_recv.at[kind, step], {"ty": ty_peer(step)})
-            for step in range(1, n_ty)
-        ]
+        return values, part, Exchange(
+            n_ty, lambda d: s_send, lambda d: s_recv.at[d], ty_send.at[kind], ty_recv.at[kind], to_ty
+        )
 
     res_e, part_e, sent_se = residual(sent_oe, x_e, o_send_e, o_recv_e, s_send_e, s_recv_e, 5)
     res_a, part_a, sent_sa = residual(sent_oa, x_a, o_send_a, o_recv_a, s_send_a, s_recv_a, 6)
 
-    partner = {"grp": 1 - grp}
-
-    def final(values, part, copies, s_recv, g_load, gain, buffer, kind):
+    def final(values, part, exchange, s_recv, g_load, gain, buffer, kind):
         width = values.shape[1]
         g_load.wait()
-        for copy, step in zip(copies, range(1, n_ty)):
-            copy.wait_recv()
-            part = part + s_recv[step]
+        part = add_up(exchange, part, s_recv)
         mean = jnp.sum(part, axis=1, keepdims=True) / (width * n_ty)
         rows = values * lax.rsqrt(mean + EPS) * gain[...].astype(F32).reshape(1, width)
         buffer[flat] = folded(rows).astype(BF16)
-        across = [
-            push(buffer.at[flat], buffer.at[flat], tx_send.at[kind, step], tx_recv.at[kind, step], {"tx": tx_peer(step)})
-            for step in range(1, n_tx)
-        ]
-        forward = [
-            push(buffer.at[flat], buffer.at[flat], fw_send.at[kind - 2, 0], fw_recv.at[kind - 2, 0], partner)
-        ]
+        across = Exchange(
+            n_tx, lambda d: buffer.at[flat], lambda d: buffer.at[flat], tx_send.at[kind], tx_recv.at[kind], to_tx
+        )
+
+        def from_tx(step):
+            return grp * n_tx + lax.rem(tx // 4 + n_tx // 4 - step // 4, n_tx // 4) * 4 + lax.rem(tx + 4 - lax.rem(step, 4), 4)
+
+        forward = Exchange(
+            n_tx, lambda d: buffer.at[from_tx(d)], lambda d: buffer.at[from_tx(d)], fw_send.at[kind - 2],
+            fw_recv.at[kind - 2], lambda d: {"grp": 1 - grp}, begin=False,
+        )
+        forward.make(0).start()
         return across, forward
 
-    def pass_on(across, forward, buffer, kind):
-        for copy, step in zip(across, range(1, n_tx)):
-            copy.wait_recv()
-            source = grp * n_tx + lax.rem(tx + n_tx - step, n_tx)
-            forward.append(
-                push(buffer.at[source], buffer.at[source], fw_send.at[kind - 2, step], fw_recv.at[kind - 2, step], partner)
-            )
-
-    def collect(forward, buffer, rows):
-        for copy in forward:
-            copy.wait_recv()
+    def collect(pair, buffer, rows):
+        across, forward = pair
+
+        @pl.loop(1, n_tx)
+        def _(step):
+            across.make(step).wait_recv()
+            forward.make(step).start()
+
+        forward.make(0).wait_recv()
+        forward.arrive()
         rows[...] = unfolded(buffer[...].astype(F32)).reshape(rows.shape).astype(BF16)
 
-    across_e, forward_e = final(res_e, part_e, sent_se, s_recv_e, l_fin_e, v_fin_e, f_e, 2)
-    across_a, forward_a = final(res_a, part_a, sent_sa, s_recv_a, l_fin_a, v_fin_a, f_a, 3)
+    pair_e = final(res_e, part_e, sent_se, s_recv_e, l_fin_e, v_fin_e, f_e, 2)
+    pair_a = final(res_a, part_a, sent_sa, s_recv_a, l_fin_a, v_fin_a, f_a, 3)
 
     padding = v_head_e.shape[0] - vocab
     l_head_e.wait()
@@ -360,37 +378,37 @@
     l_head_a.wait()
     v_head_a[pl.ds(vocab, padding), :] = jnp.zeros((padding, width_a), BF16)
 
-    n_chunk = v_head_e.shape[0] // CHUNK
-    logit_copies = []
+    n_slab = v_head_e.shape[0] // SLAB
+
+    def logit_exchange(slab, begin=True):
+        return Exchange(
+            n_ty, lambda d: l_send.at[slab, ty_peer(d)], lambda d: l_recv.at[slab, d], l_ssem.at[slab], l_rsem.at[slab],
+            to_ty, begin,
+        )
 
     def logits(rows, head, base):
-        for c in range(n_chunk):
-            part = mm_t(rows[...], head[pl.ds(c * CHUNK, CHUNK), :])
-            l_send[base + c] = part.reshape(n_ty, 16, CHUNK).astype(BF16)
-            for step in range(1, n_ty):
-                logit_copies.append(
-                    push(l_send.at[base + c, ty_peer(step)], l_recv.at[base + c, step],
-                         l_ssem.at[base + c, step], l_rsem.at[base + c, step], {"ty": ty_peer(step)})
-                )
-
-    pass_on(across_e, forward_e, f_e, 2)
-    collect(forward_e, f_e, rows_e)
+        @pl.loop(0, n_slab)
+        def _(slab):
+            for at in range(0, SLAB, CHUNK):
+                part = mm_t(rows[...], head[pl.ds(pl.multiple_of(slab * SLAB + at, CHUNK), CHUNK), :])
+                l_send[base + slab, :, :, at : at + CHUNK] = part.reshape(n_ty, 16, CHUNK).astype(BF16)
+            logit_exchange(base + slab)
+            started.pop()
+
+    collect(pair_e, f_e, rows_e)
     logits(rows_e, v_head_e, 0)
-    pass_on(across_a, forward_a, f_a, 3)
-    collect(forward_a, f_a, rows_a)
-    logits(rows_a, v_head_a, n_chunk)
-
-    def chunk_sum(c):
-        total = l_send[c, ty].astype(F32)
-        for step in range(1, n_ty):
-            logit_copies[c * (n_ty - 1) + step - 1].wait_recv()
-            total = total + l_recv[c, step].astype(F32)
-        return total
-
-    lane_c = iota((16, CHUNK), 1)
+    collect(pair_a, f_a, rows_a)
+    logits(rows_a, v_head_a, n_slab)
+
+    def slab_sum(slab):
+        exchange = logit_exchange(slab, False)
+        started.pop()
+        return add_up(exchange, l_send[slab, ty].astype(F32), l_recv.at[slab])
+
+    lane_c = iota((16, SLAB), 1)
 
     def peak_and_total(parts):
-        masked = [jnp.where(lane_c + c * CHUNK < vocab, part, -jnp.inf) for c, part in enumerate(parts)]
+        masked = [jnp.where(lane_c + c * SLAB < vocab, part, -jnp.inf) for c, part in enumerate(parts)]
         peak = masked[0]
         for part in masked[1:]:
             peak = jnp.maximum(peak, part)
@@ -406,17 +424,17 @@
     for s in range(2):
         for r in range(8):
             token = jnp.where(row16 == r // block * 8 + s * block + r % block, tokens[s, r], token)
-    token = widen(token - flat * vocab, CHUNK)
-
-    expert = [chunk_sum(c) for c in range(n_chunk)]
+    token = widen(token - flat * vocab, SLAB)
+
+    expert = [slab_sum(c) for c in range(n_slab)]
     peak_e, total_e = peak_and_total(expert)
-    amateur = [chunk_sum(n_chunk + c) for c in range(n_chunk)]
+    amateur = [slab_sum(n_slab + c) for c in range(n_slab)]
     peak_a, total_a = peak_and_total(amateur)
-    chosen = jnp.zeros((16, CHUNK), F32)
+    chosen = jnp.zeros((16, SLAB), F32)
     mixed = []
-    for c in range(n_chunk):
+    for c in range(n_slab):
         mixed.append(expert[c] - AMATEUR * amateur[c])
-        column = lane_c + c * CHUNK
+        column = lane_c + c * SLAB
         chosen = chosen + jnp.where((column == token) & (column < vocab), mixed[c], 0.0)
     chosen = jnp.sum(chosen, axis=1, keepdims=True)
 
@@ -426,11 +444,7 @@
     tile = jnp.where(lane16 == 4, chosen, tile)
     tile = jnp.where(lane8 < 64, tile[:8], tile[8:])
     t_send[...] = tile
-    copies = [
-        push(t_send, t_recv.at[step], t_ssem.at[step], t_rsem.at[step], flat_peer(step)) for step in range(1, n_flat)
-    ]
-    for copy in copies:
-        copy.wait_recv()
+    Exchange(n_flat, lambda d: t_send, lambda d: t_recv.at[d], t_ssem, t_rsem, flat_peer).arrive()
     tiles = [tile] + [t_recv[step] for step in range(1, n_flat)]
     highest = functools.reduce(jnp.maximum, tiles)
     picked = functools.reduce(jnp.add, tiles)
@@ -445,12 +459,12 @@
         return jnp.concatenate([values[:, lane : lane + 1], values[:, lane + 64 : lane + 65]], axis=0)
 
     offset = column(log_total, 0) - AMATEUR * column(log_total, 2)
-    for c in range(n_chunk):
-        size = min(CHUNK, vocab - c * CHUNK)
+    for c in range(n_slab):
+        size = min(SLAB, vocab - c * SLAB)
         contrast = mixed[c] - offset
         for s in range(2):
             low = s * block
-            out_ref[s, :, c * CHUNK : c * CHUNK + size] = jnp.concatenate(
+            out_ref[s, :, c * SLAB : c * SLAB + size] = jnp.concatenate(
                 [contrast[low : low + block], contrast[8 + low : 8 + low + block]], axis=0
             )[:, :size]
     value = jnp.broadcast_to(column(picked, 4) - offset, (16, HEAD))
@@ -460,8 +474,23 @@
         line = jnp.sum(jnp.where(mine & (lane_r < 8), value, 0.0), axis=0, keepdims=True)
         score_ref[s : s + 1, :] = line[:, :8]
 
-    for copy in sent:
-        copy.wait_send()
+    for exchange in started:
+        exchange.finish()
+    pair_e[1].make(0).wait_send()
+    pair_a[1].make(0).wait_send()
+
+    @pl.loop(0, 2 * n_slab)
+    def _(slab):
+        logit_exchange(slab, False).finish()
+        started.pop()
+
+
+def hand_over(a_in, b_in, a_out, b_out, sems):
+    copies = [pltpu.make_async_copy(a_in, a_out, sems.at[0]), pltpu.make_async_copy(b_in, b_out, sems.at[1])]
+    for copy in copies:
+        copy.start()
+    for copy in copies:
+        copy.wait()
 
 
 def on_device(axes, *args):
@@ -474,8 +503,8 @@
     n_flat = n_grp * n_tx
     half = hid_e.shape[1] // n_grp
     vocab = head_e.shape[0]
-    padded = -(-vocab // CHUNK) * CHUNK
-    n_chunk = padded // CHUNK
+    padded = -(-vocab // SLAB) * SLAB
+    n_slab = padded // SLAB
     n_rows = 2 * half
     width_e, width_a = hid_e.shape[2], hid_a.shape[2]
     cols_e = wq_e.shape[1] + wk_e.shape[1] + wv_e.shape[1]
@@ -500,7 +529,7 @@
     scratch += [
         pltpu.VMEM((n_ty, 8, width_e), F32), pltpu.VMEM((n_ty, 8, width_a), F32),
         pltpu.VMEM((8, HEAD), F32), pltpu.VMEM((n_ty, 8, HEAD), F32),
-        pltpu.VMEM((n_ty, 16, cols_e // 2), BF16), pltpu.VMEM((n_ty, 16, cols_e // 2), BF16),
+        pltpu.VMEM((n_ty, 8, cols_e), F32), pltpu.VMEM((n_ty, 8, cols_e), F32),
         pltpu.VMEM((n_ty, 16, cols_a // 2), BF16), pltpu.VMEM((n_ty, 16, cols_a // 2), BF16),
         pltpu.VMEM((n_ty, 16, inner_e // 2), BF16), pltpu.VMEM((n_ty, 16, inner_a // 2), BF16),
         pltpu.VMEM((n_tx, 16, width_e // 2), BF16), pltpu.VMEM((n_tx, 16, width_e // 2), BF16),
@@ -509,20 +538,20 @@
         pltpu.VMEM((8, HEAD), F32), pltpu.VMEM((n_ty, 8, HEAD), F32),
         pltpu.VMEM((n_flat, 16, width_e // 2), BF16), pltpu.VMEM((n_flat, 16, width_a // 2), BF16),
         pltpu.VMEM((n_flat * 8, width_e), BF16), pltpu.VMEM((n_flat * 8, width_a), BF16),
-        pltpu.VMEM((2 * n_chunk, n_ty, 16, CHUNK), BF16), pltpu.VMEM((2 * n_chunk, n_ty, 16, CHUNK), BF16),
+        pltpu.VMEM((2 * n_slab, n_ty, 16, SLAB), BF16), pltpu.VMEM((2 * n_slab, n_ty, 16, SLAB), BF16),
         pltpu.VMEM((8, HEAD), F32), pltpu.VMEM((n_flat, 8, HEAD), F32),
         pltpu.SemaphoreType.DMA((22,)),
         pltpu.SemaphoreType.DMA((7, n_ty)), pltpu.SemaphoreType.DMA((7, n_ty)),
         pltpu.SemaphoreType.DMA((4, n_tx)), pltpu.SemaphoreType.DMA((4, n_tx)),
         pltpu.SemaphoreType.DMA((2, n_tx)), pltpu.SemaphoreType.DMA((2, n_tx)),
-        pltpu.SemaphoreType.DMA((2 * n_chunk, n_ty)), pltpu.SemaphoreType.DMA((2 * n_chunk, n_ty)),
+        pltpu.SemaphoreType.DMA((2 * n_slab, n_ty)), pltpu.SemaphoreType.DMA((2 * n_slab, n_ty)),
         pltpu.SemaphoreType.DMA((n_flat,)), pltpu.SemaphoreType.DMA((n_flat,)),
     ]
     hbm = pl.BlockSpec(memory_space=pl.ANY)
     vmem = pl.BlockSpec(memory_space=pltpu.VMEM)
     macs = n_rows * (width_e * (cols_e + inner_e) + width_a * (cols_a + inner_a)) + 2 * n_rows * vocab * (width_e + width_a)
     read = sum(array.size * array.dtype.itemsize for array in args)
-    return pl.pallas_call(
+    outs = pl.pallas_call(
         functools.partial(kernel, axes, None),
         out_shape=(
             jax.ShapeDtypeStruct((2, hid_e.shape[1] // n_ty, vocab), F32),
@@ -537,6 +566,14 @@
         cost_estimate=pl.CostEstimate(flops=2 * macs, bytes_accessed=read, transcendentals=0),
         name="contrast",
     )(*args)
+    return pl.pallas_call(
+        hand_over,
+        out_shape=tuple(jax.ShapeDtypeStruct(out.shape, out.dtype) for out in outs),
+        in_specs=[hbm, hbm],
+        out_specs=(hbm, hbm),
+        scratch_shapes=[pltpu.SemaphoreType.DMA((2,))],
+        name="hand_over",
+    )(*outs)
 
 
 def solution(mesh):

time: 67.6 us -> 71.2 us (1.053)
  Pallas kernels: 64 us -> 70.4 us
  local copies, waits for them, and re-layouts: 2.8 us -> 0 us
    pallas_call x0 -> x1, Pallas kernels: none -> 5.12 us  [on_device(): pl.pallas_call(hand_over, out_shape=tuple((jax.ShapeDtypeStruct(out.shape...]
    unnamed x2 -> x0, local copies, waits for them, and re-layouts: 2.8 us -> none
    pallas_call x1, Pallas kernels: 64 us -> 65.3 us  [on_device(): pl.pallas_call(functools.partial(kernel, axes, None), out_shape=(jax.Shap...]
where the time goes in v1:
time: 71.2 us; the launch traced here: 71.1 us
  Pallas kernels  70.4 us (99%)
    pallas_call x1, Pallas kernels, on_device(): pl.pallas_call(functools.partial(kernel, axes, None), out_shape=(jax.Shap...  65.3 us
    pallas_call x1, Pallas kernels, on_device(): pl.pallas_call(hand_over, out_shape=tuple((jax.ShapeDtypeStruct(out.shape...  5.12 us

profile of v1, /device:TPU:1, one launch (start us, length us, event | category | flops | bytes accessed | tf_op | source)
XLA Modules:
  0.0 71.1 jit_solution(6477449618750203151)
XLA Ops:
  0.6 65.3 %contrast.1 = (f32[2,8,2000]{2,1,0:T(8,128)}, f32[2,8]{1,0:T(2,128)}) custom-call(bf16[2,64,1024]{2,1,0:T(8,128)(2,1)} %refs_0_.1, bf16[1024]{0:T(1024)(128)(2,1)} %refs_1_.1, bf16[1024,1024]{1,0:T(8,128)(2,1)} %refs_2_.1, bf16[1024,128]{1,0:T(8,128)(2,1)} %refs_3_.1, bf16[1024,128]{1,0:T(8,128)(2,1)} %refs_4_.1, bf16[1024,1024]{1,0:T(8,128)(2,1)} %refs_5_.1, ...), custom_call_target="tpu_custom_call" | custom-call | flops 1222639616 | bytes 23844944 | tf_op jit(solution)/shard_map/contrast/pallas_call | solution.py:554
  66.0 5.1 %hand_over.1 = (f32[2,8,2000]{2,1,0:T(8,128)}, f32[2,8]{1,0:T(2,128)}) custom-call(f32[2,8,2000]{2,1,0:T(8,128)} %get-tuple-element.4.a_in, f32[2,8]{1,0:T(2,128)} %get-tuple-element.5.b_in), custom_call_target="tpu_custom_call" | custom-call | tf_op jit(solution)/shard_map/hand_over/pallas_call | solution.py:569
